TPU v7x, 512 devices: a whole 4x8x8 slice. The times are simulated.
512 devices in a mesh: rep: 128 (over z, y, x_lo), tp: 4 (over x_hi, core).
Axes of the slice: x: 4 (x_hi: 2, x_lo: 2; x = x_hi * 2 + x_lo), y: 8, z: 8, core: 2. Of those that a mesh axis runs over, the one named last changes fastest.
Arguments:
- tokens: bfloat16 [16384, 2560], P('rep', 'tp'), may hold values from -6 to 6
- weights: bfloat16 [128, 2560, 1728], P('rep', 'tp'), may hold values from -6 to 6
- push_scale: bfloat16 [128, 4], P('rep', 'tp'), may hold values from 0.5 to 2
- cotangent: bfloat16 [128, 1728, 512], P('rep', 'tp'), may hold values from -6 to 6
- step_count: int32 [1], replicated, may hold values from 0 to 999
Outputs:
- mixed_weights: bfloat16 [128, 2560, 1728], P('rep', 'tp')
- mixed_scale: float32 [128, 4], P('rep', 'tp')
All inputs are finite; a program needn't handle non-finite values.
Results may differ from a plain program's by a relative error of at most 0.006.
Values may be sent and summed in bfloat16 or wider, within the bound.
A program may use at most 128 MiB of HBM per device.

v0:
```python
import math

import jax
import jax.numpy as jnp
from jax import lax
from jax.sharding import PartitionSpec as P

learning_rate = 0.5


def from_partner(value, axis, distance):
    return lax.ppermute(value, axis, [(i, i ^ 1 << distance) for i in range(lax.axis_size(axis))])


def for_sending(value):

    def short(part):
        return part.astype(jnp.bfloat16) if part.dtype == jnp.float32 else part

    return jax.tree.map(short, value)


def from_behind(value, axis, steps):
    count = lax.axis_size(axis)
    pairs = [(source, (source + steps) % count) for source in range(count)]
    return lax.ppermute(value, axis, pairs)


def silu_slope(hidden):
    sigma = jax.nn.sigmoid(hidden)
    return sigma * (1.0 + hidden * (1.0 - sigma))


def weight_grad(token_rows, slopes, inverse):
    return (
        lax.dot_general(
            token_rows, slopes, (((0,), (1,)), ((), ())), preferred_element_type=jnp.float32
        )
        * inverse
    )


def join_rows(block, bit_number):
    partner = from_partner(block, "rep", bit_number)
    is_lower = lax.axis_index("rep") // 2**bit_number % 2 == 0
    return jnp.where(
        is_lower, jnp.concatenate([block, partner], 1), jnp.concatenate([partner, block], 1)
    )


def shift_updated(payload, chosen_level, levels):

    def build_branch(distance):
        return lambda parcel: from_behind(
            (for_sending(parcel[0]), for_sending(parcel[1])), "rep", distance
        )

    return lax.switch(
        chosen_level, [build_branch(2 ** (number + 2)) for number in range(levels)], payload
    )


def per_device(tokens, weights, push_scale, cotangent, step_count):
    model_width = tokens.shape[1] * lax.axis_size("tp")
    inverse = 1.0 / math.sqrt(model_width)
    levels = lax.axis_size("rep").bit_length() - 3
    chosen_level = step_count[0] % levels
    row_blocks = tokens[None]
    weight_list = weights[0]
    cot_list = cotangent[0]
    for bit_number in range(2):
        row_blocks = join_rows(row_blocks, bit_number)
    scaled_list = (weight_list.astype(jnp.float32) / push_scale[0, 0].astype(jnp.float32)).astype(
        jnp.bfloat16
    )
    contract = (((0,), (1,)), ((), ()))
    partial_sum = lax.dot_general(
        scaled_list, row_blocks[0], contract, preferred_element_type=jnp.float32
    )
    hidden = lax.psum(partial_sum.astype(jnp.bfloat16), "tp").astype(jnp.float32) * inverse
    cot_full = lax.all_gather(cot_list, "tp", axis=0, tiled=True)
    slope_all = (cot_full.astype(jnp.float32) * silu_slope(hidden)).astype(jnp.bfloat16)
    stepped_list = (
        weight_list.astype(jnp.float32)
        - learning_rate * weight_grad(row_blocks[0], slope_all, inverse)
    ).astype(jnp.bfloat16)
    source_stepped, source_scale = shift_updated((stepped_list, push_scale), chosen_level, levels)
    mixed_weights = (
        0.5 * (stepped_list.astype(jnp.float32) + source_stepped.astype(jnp.float32))
    ).astype(jnp.bfloat16)
    mixed_scale = 0.5 * (push_scale.astype(jnp.float32) + source_scale.astype(jnp.float32))
    return (mixed_weights[None], mixed_scale)


def solution(mesh):
    placed = (P("rep", "tp"), P("rep", "tp", None), P("rep", "tp"), P("rep", "tp", None), P())
    return jax.shard_map(
        per_device,
        mesh=mesh,
        in_specs=placed,
        out_specs=(P("rep", "tp", None), P("rep", "tp")),
        check_vma=False,
    )
```

profile of v0, /device:TPU:24, one launch (start us, length us, event | category | flops | bytes accessed | tf_op | source)
XLA Modules:
  0.0 254.3 jit_solution(3841555651126664807)
XLA Ops:
  7.2 0.0 all-reduce.2.cloned.1.call-start
  7.2 3.4 %collective-permute-start.10 = (bf16[1,128,640]{2,1,0:T(8,128)(2,1)}, bf16[1,128,640]{2,1,0:T(8,128)(2,1)S(1)}, u32[]{:S(2)}, u32[]{:S(2)}) collective-permute-start(bf16[1,128,640]{2,1,0:T(8,128)(2,1)} %bitcast.18), channel_id=1, source_target_pairs={{0,4},{4,0},{8,12},{12,8},{16,20},{20,16},{24,28},{28,24},{32,36},... | collective-permute-start | bytes 491528 | tf_op jit(solution)/shard_map/ppermute | solution.py:12
  10.6 4.6 %collective-permute-done.10 = bf16[1,128,640]{2,1,0:T(8,128)(2,1)S(1)} collective-permute-done((bf16[1,128,640]{2,1,0:T(8,128)(2,1)}, bf16[1,128,640]{2,1,0:T(8,128)(2,1)S(1)}, u32[]{:S(2)}, u32[]{:S(2)}) %collective-permute-start.10) | collective-permute-done | bytes 163872 | tf_op jit(solution)/shard_map/ppermute | solution.py:12
  15.3 1.1 maximum_select_fusion.2
  16.3 2.4 collective-permute-start.11
  19.4 1.1 maximum_select_fusion.1
  20.5 6.3 %collective-permute-done.11 = bf16[1,256,640]{2,1,0:T(8,128)(2,1)S(1)} collective-permute-done((bf16[1,256,640]{2,1,0:T(8,128)(2,1)S(1)}, bf16[1,256,640]{2,1,0:T(8,128)(2,1)S(1)}, u32[]{:S(2)}, u32[]{:S(2)}) %collective-permute-start.11) | collective-permute-done | bytes 327712 | tf_op jit(solution)/shard_map/ppermute | solution.py:12
  26.8 4.4 %convolution_convert_fusion = bf16[1728,512]{1,0:T(8,128)(2,1)} fusion(bf16[1,640,1728]{1,2,0:T(8,128)(2,1)} %param.11, f32[]{:T(128)} %bitcast.6, bf16[256,640]{1,0:T(8,128)(2,1)S(1)} %bitcast.21, bf16[256,640]{1,0:T(8,128)(2,1)S(1)} %maximum_select_fusion.1, pred[]{:T(512)S(6)} %eq.10), kind=kOutput, calls=%fused_computation.9 | convolution fusion | flops 1139613696 | bytes 4636677 | tf_op jit(solution)/shard_map/dot_general | solution.py:77
  31.2 0.0 all-reduce.2.cloned.1.call-update
  31.2 0.0 all-gather.3.cloned.1.call-start
  31.3 0.7 all-gather.3.cloned.1.call-update
  32.7 67.9 %all-reduce.2.cloned.1.call-done = bf16[1728,512]{1,0:T(8,128)(2,1)} async-done(((bf16[1728,512]{1,0:T(8,128)(2,1)}), bf16[1728,512]{1,0:T(8,128)(2,1)}) %all-reduce.2.cloned.1.call-update) | async-done | bytes 1769488 | tf_op jit(solution)/shard_map/psum | solution.py:80
  100.5 32.0 %all-gather.3.cloned.1.call-done = bf16[1,1728,512]{2,1,0:T(8,128)(2,1)} async-done(((bf16[1,432,512]{2,1,0:T(8,128)(2,1)}), bf16[1,1728,512]{2,1,0:T(8,128)(2,1)}) %all-gather.3.cloned.1.call-update) | async-done | bytes 1769488 | tf_op jit(solution)/shard_map/all_gather | solution.py:81
  132.5 5.6 %fusion.1 = bf16[640,1728]{0,1:T(8,128)(2,1)S(1)} fusion(bf16[1,640,1728]{1,2,0:T(8,128)(2,1)} %param.11, bf16[1728,512]{1,0:T(8,128)(2,1)} %all-reduce.2.cloned.1.call-done, bf16[1,1728,512]{2,1,0:T(8,128)(2,1)} %all-gather.3.cloned.1.call-done, bf16[256,640]{1,0:T(8,128)(2,1)S(1)} %bitcast.22, bf16[256,640]{1,0:T(8,128)(2,1)S(1)} %maximum_select_fusion.1, ...), kind=kOutput, calls=%fused_computation.3 | convolution fusion | flops 1150451712 | bytes 8617985 | tf_op jit(solution)/shard_map/dot_general | solution.py:36
  138.1 103.9 %conditional.4 = (bf16[640,1728]{0,1:T(8,128)(2,1)}, bf16[1,1]{1,0:T(2,128)(2,1)}) conditional(s32[]{:T(128)} %clamp.3, (bf16[640,1728]{0,1:T(8,128)(2,1)S(1)}, bf16[1,1]{1,0:T(2,128)(2,1)}) %tuple.60, (bf16[640,1728]{0,1:T(8,128)(2,1)S(1)}, bf16[1,1]{1,0:T(2,128)(2,1)}) %tuple.60, (bf16[640,1728]{0,1:T(8,128)(2,1)S(1)}, ...), branch_computations={%region_1.2_spmd, %region_2.3_spmd, %region_3.4_spmd, %region_4.5_... | conditional | bytes 8847464
  138.2 8.0 %collective-permute-start.8 = (bf16[640,1728]{0,1:T(8,128)(2,1)S(1)}, bf16[640,1728]{0,1:T(8,128)(2,1)}, u32[]{:S(2)}, u32[]{:S(2)}) collective-permute-start(bf16[640,1728]{0,1:T(8,128)(2,1)S(1)} %get-tuple-element.40), channel_id=1, source_target_pairs={{0,256},{4,260},{8,264},{12,268},{16,272},{20,276},{24,280},{28,28... | collective-permute-start | bytes 6635528 | tf_op jit(solution)/shard_map/cond/branch_4_fun/ppermute | solution.py:26
  146.2 1.9 collective-permute-start.9
  148.1 93.9 %collective-permute-done.9 = bf16[1,1]{1,0:T(2,128)(2,1)} collective-permute-done((bf16[1,1]{1,0:T(2,128)(2,1)}, bf16[1,1]{1,0:T(2,128)(2,1)}, u32[]{:S(2)}, u32[]{:S(2)}) %collective-permute-start.9) | collective-permute-done | bytes 34 | tf_op jit(solution)/shard_map/cond/branch_4_fun/ppermute | solution.py:26
  242.0 0.0 collective-permute-done.8
  242.7 3.7 %fusion.5 = bf16[1,640,1728]{1,2,0:T(8,128)(2,1)} fusion(bf16[640,1728]{0,1:T(8,128)(2,1)} %get-tuple-element.62, bf16[640,1728]{0,1:T(8,128)(2,1)S(1)} %fusion.1), kind=kLoop, calls=%fused_computation.10 | loop fusion | flops 5529600 | bytes 6635520 | tf_op jit(solution)/shard_map/broadcast_in_dim | solution.py:92
Async XLA Ops:
  7.2 93.4 %all-reduce.2.cloned.1.call-start = ((), (), s32[]{:S(2)}) async-start(), calls=%async_computation | async-start | bytes 3538944 | tf_op jit(solution)/shard_map/psum | solution.py:80
  7.2 8.0 %collective-permute-start.10 = (bf16[1,128,640]{2,1,0:T(8,128)(2,1)}, bf16[1,128,640]{2,1,0:T(8,128)(2,1)S(1)}, u32[]{:S(2)}, u32[]{:S(2)}) collective-permute-start(bf16[1,128,640]{2,1,0:T(8,128)(2,1)} %bitcast.18), channel_id=1, source_target_pairs={{0,4},{4,0},{8,12},{12,8},{16,20},{20,16},{24,28},{28,24},{32,36},... | collective-permute-start | bytes 491528 | tf_op jit(solution)/shard_map/ppermute | solution.py:12
  16.3 10.5 %collective-permute-start.11 = (bf16[1,256,640]{2,1,0:T(8,128)(2,1)S(1)}, bf16[1,256,640]{2,1,0:T(8,128)(2,1)S(1)}, u32[]{:S(2)}, u32[]{:S(2)}) collective-permute-start(bf16[1,256,640]{2,1,0:T(8,128)(2,1)S(1)} %maximum_select_fusion.2), channel_id=1, source_target_pairs={{0,8},{4,12},{8,0},{12,4},{16,24},{20,28},{24,16},{28,20},{32,40},... | collective-permute-start | bytes 983048 | tf_op jit(solution)/shard_map/ppermute | solution.py:12
  31.2 101.3 %all-gather.3.cloned.1.call-start = ((), (), s32[]{:S(2)}) async-start(), calls=%async_computation.1 | async-start | bytes 2211840 | tf_op jit(solution)/shard_map/all_gather | solution.py:81
  138.2 103.9 %collective-permute-start.8 = (bf16[640,1728]{0,1:T(8,128)(2,1)S(1)}, bf16[640,1728]{0,1:T(8,128)(2,1)}, u32[]{:S(2)}, u32[]{:S(2)}) collective-permute-start(bf16[640,1728]{0,1:T(8,128)(2,1)S(1)} %get-tuple-element.40), channel_id=1, source_target_pairs={{0,256},{4,260},{8,264},{12,268},{16,272},{20,276},{24,280},{28,28... | collective-permute-start | bytes 6635528 | tf_op jit(solution)/shard_map/cond/branch_4_fun/ppermute | solution.py:26
  146.2 95.8 %collective-permute-start.9 = (bf16[1,1]{1,0:T(2,128)(2,1)}, bf16[1,1]{1,0:T(2,128)(2,1)}, u32[]{:S(2)}, u32[]{:S(2)}) collective-permute-start(bf16[1,1]{1,0:T(2,128)(2,1)} %get-tuple-element.41), channel_id=1, source_target_pairs={{0,256},{4,260},{8,264},{12,268},{16,272},{20,276},{24,280},{28,28... | collective-permute-start | bytes 14 | tf_op jit(solution)/shard_map/cond/branch_4_fun/ppermute | solution.py:26
Sparse Core Ops, SparseCore 0:
  31.4 69.1 all-reduce.1
  102.9 29.6 all-gather.2
where the time goes:
time: 255 us; the launch traced here: 254 us
  waiting for transfers between devices  205 us (80%)
  between operations  17.3 us (7%)
  starting transfers between devices  15.8 us (6%)
  matrix products  10 us (4%)
  other arithmetic  5.82 us (2%)
    ppermute x2, waiting for transfers between devices, from_behind(): return lax.ppermute(value, axis, pairs)  93.9 us
    psum x1, waiting for transfers between devices, per_device(): lax.psum(partial_sum.astype(jnp.bfloat16), 'tp').astype(jnp.float32)  67.9 us
    all_gather x1, waiting for transfers between devices, per_device(): cot_full = lax.all_gather(cot_list, 'tp', axis=0, tiled=True)  32 us
    ppermute x2, waiting for transfers between devices, from_partner(): lax.ppermute(value, axis, [(i, i ^ 1 << distance) for i in range(lax.axis...  11 us
    ppermute x2, starting transfers between devices, from_behind(): return lax.ppermute(value, axis, pairs)  9.93 us
    ppermute x2, starting transfers between devices, from_partner(): lax.ppermute(value, axis, [(i, i ^ 1 << distance) for i in range(lax.axis...  5.76 us
    dot_general x1, matrix products, weight_grad(): lax.dot_general(token_rows, slopes, (((0,), (1,)), ((), ())), preferred_e...  5.6 us
  transfers between devices with their start and end apart: 6, of which 5 were waited for; matrix products, arithmetic and copies ran while one was open for 0% of the time, Pallas kernels for 0%

commit v1 on v0

v1 whole, which is shorter than its diff:
```python
import functools
import math

import jax
import jax.numpy as jnp
from jax import lax
from jax.experimental import pallas as pl
from jax.experimental.pallas import tpu as pltpu
from jax.sharding import PartitionSpec as P

learning_rate = 0.5
MESH = pl.DeviceIdType.MESH
CHUNKS = (48, 96, 144, 144)
STARTS = tuple(sum(CHUNKS[:i]) for i in range(len(CHUNKS)))
RELAYED = ((3,), (3,), (2, 3), ())
LANES = 128


def moved(rep, dz, dy):
    z, y, x = rep // 16, rep // 2 % 8, rep % 2
    return (z + dz + 8) % 8 * 16 + (y + dy + 8) % 8 * 2 + x


def kernel(
    level,
    inverse,
    tok_hbm,
    w_hbm,
    scale_ref,
    cot_hbm,
    out_hbm,
    mixed_scale_ref,
    w,
    xt,
    tok,
    cot,
    part,
    part_rx,
    slope,
    rx,
    relay,
    out,
    sc_own,
    sc_rx,
    load_sem,
    tok_s,
    tok_r,
    rs_s,
    rs_r,
    ag_s,
    ag_r,
    mx_s,
    mx_r,
    rl_r,
    fw_s,
    sc_sem,
    out_sem,
):
    rep, tp = lax.axis_index("rep"), lax.axis_index("tp")
    n_rep, n_tp = lax.axis_size("rep"), lax.axis_size("tp")
    rows, width = tok_hbm.shape
    hidden_units = w_hbm.shape[1]
    share = hidden_units // n_tp
    count = len(CHUNKS)
    shift = 4 * 2**level
    relayed = RELAYED if level in (0, 3) else ((),) * count
    back = (0, 3) if level == 0 else (3, 0)

    member = rep % 4
    flip1 = 1 - 2 * (member % 2)
    flip2 = 2 - 4 * (member // 2)
    mates = [rep + flip1, rep + flip2, rep + flip1 + flip2]
    target = (rep + shift) % n_rep
    origin = (rep + n_rep - shift) % n_rep
    via = moved(rep, -back[0], -back[1])
    from_via = moved(rep, back[0], back[1])
    via_target = (from_via + shift) % n_rep
    last_via = moved(origin, -back[0], -back[1])

    loads = [
        pltpu.make_async_copy(w_hbm, w, load_sem.at[0]),
        pltpu.make_async_copy(
            tok_hbm, tok.at[pl.ds(pl.multiple_of(member * rows, rows), rows)], load_sem.at[1]
        ),
        pltpu.make_async_copy(cot_hbm, cot, load_sem.at[2]),
    ]
    for load in loads:
        load.start()

    senders = [(m, tp) for m in mates]
    senders += [(rep, (tp + n_tp - q) % n_tp) for q in (1, 2, 3)]
    senders += [(origin, tp)]
    if any(relayed):
        senders += [(from_via, tp), (last_via, tp)]
    barrier = pltpu.get_barrier_semaphore()
    for sender in senders:
        pl.semaphore_signal(barrier, inc=1, device_id=sender, device_id_type=MESH)
    scale = scale_ref[...].astype(jnp.float32)
    sc_own[...] = jnp.broadcast_to(scale, sc_own.shape)
    pl.semaphore_wait(barrier, len(senders))

    def send(src, dst, s, r, to):
        return pltpu.make_async_remote_copy(
            src_ref=src, dst_ref=dst, send_sem=s, recv_sem=r, device_id=to, device_id_type=MESH
        )

    own_rows = pl.ds(pl.multiple_of(member * rows, rows), rows)
    tok_copies = [
        send(tok_hbm, tok.at[own_rows], tok_s.at[i], tok_r.at[i], (m, tp))
        for i, m in enumerate(mates)
    ]
    for copy in tok_copies:
        copy.start()
    sc_copy = send(sc_own, sc_rx, sc_sem.at[0], sc_sem.at[1], (target, tp))
    sc_copy.start()

    full = hidden_units // LANES
    with jax.named_scope("transpose_in"):
        loads[0].wait()

        def turn(i, _):
            at = pl.ds(pl.multiple_of(i * LANES, LANES), LANES)
            xt[at, :] = w[:, at].T
            return 0

        lax.fori_loop(0, full, turn, 0)
        if hidden_units % LANES:
            xt[full * LANES :, :] = w[:, full * LANES :].T

    with jax.named_scope("wait_tokens"):
        loads[1].wait()
        for copy in tok_copies:
            copy.wait_recv()

    factor = inverse / scale

    def piece(owner, k):
        return pl.ds(pl.multiple_of(owner * share + STARTS[k], 16), CHUNKS[k])

    def rs_copy(k, q):
        to = (tp + q) % n_tp
        return send(
            part.at[piece(to, k)],
            part_rx.at[q - 1, pl.ds(STARTS[k], CHUNKS[k])],
            rs_s.at[k, q - 1],
            rs_r.at[k, q - 1],
            (rep, to),
        )

    def ag_copy(k, q, owner):
        return send(
            slope.at[piece(owner, k)],
            slope.at[piece(owner, k)],
            ag_s.at[k, q - 1],
            ag_r.at[k, q - 1],
            (rep, (tp + q) % n_tp),
        )

    def mix_copy(k, u):
        at = piece(u, k)
        if u in relayed[k]:
            return send(xt.at[at], relay.at[at], mx_s.at[k, u], rl_r.at[k, u], (via, tp))
        return send(xt.at[at], rx.at[at], mx_s.at[k, u], mx_r.at[k, u], (target, tp))

    def forward_copy(k, u):
        at = piece(u, k)
        return send(relay.at[at], rx.at[at], fw_s.at[k, u], mx_r.at[k, u], (via_target, tp))

    def products(k):
        with jax.named_scope("products"):

            def one(u, _):
                at = piece(u, k)
                p = lax.dot_general(
                    xt[at, :], tok[...], (((1,), (1,)), ((), ())), preferred_element_type=jnp.float32
                )
                part[at, :] = (p * factor).astype(jnp.bfloat16)
                return 0

            lax.fori_loop(0, n_tp, one, 0)

    def scatter(k):
        for q in (2, 1, 3):
            rs_copy(k, q).start()

    def slopes(k):
        with jax.named_scope("slopes"):
            for q in (1, 2, 3):
                rs_copy(k, q).wait_recv()
            mine = piece(tp, k)
            local = pl.ds(STARTS[k], CHUNKS[k])
            h = part[mine, :].astype(jnp.float32)
            for q in range(3):
                h += part_rx[q, local, :].astype(jnp.float32)
            sigma = jax.nn.sigmoid(h)
            d = sigma * (1.0 + h * (1.0 - sigma))
            slope[mine, :] = (cot[local, :].astype(jnp.float32) * d).astype(jnp.bfloat16)
            for q in (2, 1, 3):
                ag_copy(k, q, tp).start()

    def step(k):
        with jax.named_scope("step"):
            for q in (1, 2, 3):
                ag_copy(k, q, (tp + n_tp - q) % n_tp).wait_recv()
            for u in range(n_tp):
                at = piece(u, k)
                g = jnp.dot(slope[at, :], tok[...], preferred_element_type=jnp.float32)
                x = xt[at, :].astype(jnp.float32)
                xt[at, :] = (x - (learning_rate * inverse) * g).astype(jnp.bfloat16)
                mix_copy(k, u).start()

    def forward(k):
        for u in relayed[k]:
            with jax.named_scope("forward"):
                send(
                    relay.at[piece(u, k)], relay.at[piece(u, k)], fw_s.at[k, u], rl_r.at[k, u], (via, tp)
                ).wait_recv()
                forward_copy(k, u).start()

    products(0)
    scatter(0)
    products(1)
    loads[2].wait()
    slopes(0)
    scatter(1)
    for k in range(count):
        step(k)
        if k + 2 < count:
            products(k + 2)
        if k + 1 < count:
            slopes(k + 1)
        if k + 2 < count:
            scatter(k + 2)
        if k >= 1:
            forward(k - 1)
    forward(count - 1)

    blocks = [(i, min(i + LANES, hidden_units)) for i in range(0, hidden_units, LANES)]
    arrived = set()
    done = set()
    sc_copy.wait()
    mixed_scale_ref[...] = (0.5 * (sc_own[...] + sc_rx[...]))[:1, :1]
    for k in range(count):
        for u in range(n_tp):
            with jax.named_scope("wait_mix"):
                send(
                    rx.at[piece(u, k)], rx.at[piece(u, k)], mx_s.at[k, u], mx_r.at[k, u], (target, tp)
                ).wait_recv()
            begin = u * share + STARTS[k]
            arrived.update(range(begin, begin + CHUNKS[k], 16))
            for a, b in blocks:
                if a not in done and arrived.issuperset(range(a, b, 16)):
                    done.add(a)
                    with jax.named_scope("mix"):
                        m = 0.5 * (xt[a:b, :].astype(jnp.float32) + rx[a:b, :].astype(jnp.float32))
                        out[:, a:b] = m.astype(jnp.bfloat16).T
    store = pltpu.make_async_copy(out, out_hbm, out_sem)
    store.start()

    for copy in tok_copies:
        copy.wait_send()
    loads_left = []
    for k in range(count):
        for q in (1, 2, 3):
            rs_copy(k, q).wait_send()
            ag_copy(k, q, tp).wait_send()
        for u in range(n_tp):
            mix_copy(k, u).wait_send()
        for u in relayed[k]:
            forward_copy(k, u).wait_send()
    store.wait()


def one_level(level, inverse, tokens, weights, push_scale, cotangent):
    rows, width = tokens.shape
    hidden_units = weights.shape[1]
    share, all_tokens = cotangent.shape
    count = len(CHUNKS)
    half, single = jnp.bfloat16, jnp.float32
    dma = pltpu.SemaphoreType.DMA
    anywhere, vmem = pl.BlockSpec(memory_space=pl.ANY), pl.BlockSpec(memory_space=pltpu.VMEM)
    return pl.pallas_call(
        functools.partial(kernel, level, inverse),
        out_shape=(
            jax.ShapeDtypeStruct((width, hidden_units), half),
            jax.ShapeDtypeStruct((1, 1), single),
        ),
        in_specs=[anywhere, anywhere, vmem, anywhere],
        out_specs=(anywhere, vmem),
        scratch_shapes=[
            pltpu.VMEM((width, hidden_units), half),
            pltpu.VMEM((hidden_units, width), half),
            pltpu.VMEM((all_tokens, width), half),
            pltpu.VMEM((share, all_tokens), half),
            pltpu.VMEM((hidden_units, all_tokens), half),
            pltpu.VMEM((3, share, all_tokens), half),
            pltpu.VMEM((hidden_units, all_tokens), half),
            pltpu.VMEM((hidden_units, width), half),
            pltpu.VMEM((hidden_units, width), half),
            pltpu.VMEM((width, hidden_units), half),
            pltpu.VMEM((8, LANES), single),
            pltpu.VMEM((8, LANES), single),
            dma((3,)),
            dma((3,)),
            dma((3,)),
            dma((count, 3)),
            dma((count, 3)),
            dma((count, 3)),
            dma((count, 3)),
            dma((count, 4)),
            dma((count, 4)),
            dma((count, 4)),
            dma((count, 4)),
            dma((2,)),
            dma,
        ],
        compiler_params=pltpu.CompilerParams(
            collective_id=level, has_side_effects=True, vmem_limit_bytes=48 * 2**20
        ),
        cost_estimate=pl.CostEstimate(
            flops=4 * width * hidden_units * all_tokens,
            bytes_accessed=8 * width * hidden_units,
            transcendentals=share * all_tokens,
        ),
        name="push_step",
    )(tokens, weights, push_scale, cotangent)


def per_device(tokens, weights, push_scale, cotangent, step_count):
    inverse = 1.0 / math.sqrt(tokens.shape[1] * lax.axis_size("tp"))
    levels = lax.axis_size("rep").bit_length() - 3
    mixed, mixed_scale = lax.switch(
        step_count[0] % levels,
        [functools.partial(one_level, level, inverse) for level in range(levels)],
        tokens,
        weights[0],
        push_scale,
        cotangent[0],
    )
    return mixed[None], mixed_scale


def solution(mesh):
    placed = (P("rep", "tp"), P("rep", "tp", None), P("rep", "tp"), P("rep", "tp", None), P())
    return jax.shard_map(
        per_device,
        mesh=mesh,
        in_specs=placed,
        out_specs=(P("rep", "tp", None), P("rep", "tp")),
        check_vma=False,
    )
```

time: 255 us -> 149 us (0.58)
  the two profiles are of different devices: /device:TPU:24 before, /device:TPU:13 now
where the time goes in v1:
time: 149 us
  Pallas kernels  139 us (93%)
  local copies, waits for them, and re-layouts  6.83 us (5%)
  between operations  3.13 us (2%)
    pallas_call x1, Pallas kernels, one_level(): pl.pallas_call(functools.partial(kernel, level, inverse), out_shape=(jax....  139 us
    unnamed x5, local copies, waits for them, and re-layouts  4.35 us

profile of v1, /device:TPU:13, one launch (start us, length us, event | category | flops | bytes accessed | tf_op | source)
XLA Modules:
  0.0 149.1 jit_solution(4813815126668880839)
XLA Ops:
  1.3 0.0 copy-start
  1.3 0.0 copy-start.1
  1.3 4.3 %copy.7 = bf16[1,640,1728]{2,1,0:T(8,128)(2,1)} copy(bf16[1,640,1728]{1,2,0:T(8,128)(2,1)} %param.11) | data formatting | bytes 4423680 | tf_op args[1]
  5.7 0.0 copy-done
  5.7 0.0 copy-done.1
  5.7 141.6 %conditional.1 = (f32[1,1]{1,0:T(1,128)}, bf16[1,640,1728]{1,2,0:T(8,128)(2,1)}) conditional(s32[]{:T(128)} %clamp.3, (bf16[128,640]{1,0:T(8,128)(2,1)S(1)}, bf16[640,1728]{1,0:T(8,128)(2,1)}, bf16[1,1]{1,0:T(2,128)(2,1)}, bf16[432,512]{1,0:T(8,128)(2,1)S(1)}) %tuple.58, (bf16[128,640]{1,0:T(8,128)(2,1)S(1)}, ...), branch_computations={%region_0.1_spmd, %region_1.2_spmd, %region_2.3_spmd, %region_3.4_... | conditional | flops 2264924160 | bytes 13271056 | solution.py:332
  5.7 139.1 %push_step.6 = (bf16[640,1728]{1,0:T(8,128)(2,1)S(1)}, f32[1,1]{1,0:T(1,128)}) custom-call(bf16[128,640]{1,0:T(8,128)(2,1)S(1)} %get-tuple-element.57.tok_hbm, bf16[640,1728]{1,0:T(8,128)(2,1)} %get-tuple-element.58.w_hbm, bf16[1,1]{1,0:T(2,128)(2,1)} %get-tuple-element.59.scale_ref, bf16[432,512]{1,0:T(8,128)(2,1)S(1)} %get-tuple-element.60.cot_hbm), custom_call_target="tpu_custom_call" | custom-call | flops 2264924160 | bytes 8847360 | tf_op jit(solution)/shard_map/cond/branch_1_fun/push_step/pallas_call | solution.py:282
  144.8 2.5 %copy.10 = bf16[1,640,1728]{1,2,0:T(8,128)(2,1)} copy(bf16[1,640,1728]{2,1,0:T(8,128)(2,1)S(1)} %bitcast.9) | data formatting | bytes 4423680 | tf_op jit(solution)/shard_map/cond
Async XLA Ops:
  1.3 4.4 %copy-start = (bf16[1,432,512]{2,1,0:T(8,128)(2,1)S(1)}, bf16[1,432,512]{2,1,0:T(8,128)(2,1)}, u32[]{:S(2)}) copy-start(bf16[1,432,512]{2,1,0:T(8,128)(2,1)} %param.13) | copy-start | bytes 1327108
  1.3 4.4 %copy-start.1 = (bf16[128,640]{1,0:T(8,128)(2,1)S(1)}, bf16[128,640]{1,0:T(8,128)(2,1)}, u32[]{:S(2)}) copy-start(bf16[128,640]{1,0:T(8,128)(2,1)} %param.10) | copy-start | bytes 491524
